TPU v7x, 512 devices: a whole 4x4x16 slice. The times are simulated.
512 devices in a mesh: gx: 4 (over z_lo), gy: 16 (over x, z_hi), gz: 8 (over y, core).
Axes of the slice: x: 4, y: 4, z: 16 (z_hi: 4, z_lo: 4; z = z_hi * 4 + z_lo), core: 2. Of those that a mesh axis runs over, the one named last changes fastest.
Arguments:
- e_field: float32 [3, 32, 128, 2048], P(None, 'gz', 'gx', 'gy'), may hold values from -6 to 6
- h_field: float32 [3, 32, 128, 2048], P(None, 'gz', 'gx', 'gy'), may hold values from -6 to 6
- pole_current: float32 [3, 32, 128, 2048], P(None, 'gz', 'gx', 'gy'), may hold values from -6 to 6
- material: int32 [32, 128, 2048], P('gz', 'gx', 'gy'), may hold values from 0 to 3
- pole_table: float32 [3, 4], replicated, may hold values from 0.2 to 0.9
- cotangent: float32 [16, 8, 4096], P(None, None, ('gx', 'gy', 'gz')), may hold values from -6 to 6
- cosines: float32 [2, 4096], P(None, ('gx', 'gy', 'gz')), may hold values from -0.7 to 0.7
- wavenumber: float32 [16], replicated, may hold values from 0.6 to 0.8
- time_phase: float32 [16], replicated, may hold values from -3.140625 to 3.140625
Outputs:
- e_next: float32 [3, 32, 128, 2048], P(None, 'gz', 'gx', 'gy')
- h_next: float32 [3, 32, 128, 2048], P(None, 'gz', 'gx', 'gy')
- pole_next: float32 [3, 32, 128, 2048], P(None, 'gz', 'gx', 'gy')
All inputs are finite; a program needn't handle non-finite values.
Results may differ from a plain program's by a relative error of at most 0.0003.
Values sent between devices are 32-bit elements; how exact they have to be, the bound alone decides.
A program may use at most 64 MiB of HBM per device.

v0:
```python
import math
import jax
import jax.numpy as jnp
from jax import lax
from jax.sharding import PartitionSpec as P

FREQS = 16
DIRS = 4096
NPOLE = 4
courant = 0.5


def turned_gather(arrays, axis, dims):
    turned = [jnp.moveaxis(a, dim, 0) for a, dim in zip(arrays, dims)]
    widths = [t[0].size for t in turned]
    both = jnp.concatenate([t.reshape(-1, w) for t, w in zip(turned, widths)], axis=1)
    filled = lax.all_gather(both, axis, axis=0, tiled=True)
    tiles = jnp.split(filled, [sum(widths[:k]) for k in range(1, len(widths))], axis=1)
    return tuple(
        (
            jnp.moveaxis(b.reshape(-1, *t.shape[1:]), 0, dim)
            for b, t, dim in zip(tiles, turned, dims)
        )
    )


def copy_for_each(array, axis):
    copies = jnp.broadcast_to(array, (lax.axis_size(axis), *array.shape))
    return lax.all_to_all(copies, axis, split_axis=0, concat_axis=0, tiled=True)


def of_everyone(array, axis):
    return copy_for_each(array, axis).sum(axis=0)


def from_behind(array, axis, by):
    size = lax.axis_size(axis)
    pairs = [(i, i + by) for i in range(size) if 0 <= i + by < size]
    return lax.ppermute(array, axis, pairs)


def surface_source(cotangent, cosines, wavenumber, time_phase, xs, ys):
    count = cotangent.shape[2]
    rows_x = xs.shape[0]
    rows_y = ys.shape[0]

    def one_freq(total, freq):
        wave = wavenumber[freq]
        along_x = wave * cosines[0]
        along_y = wave * cosines[1]
        phase_x = xs[:, None] * along_x[None, :] - time_phase[freq]
        phase_y = ys[:, None] * along_y[None, :]
        cos_x = jnp.cos(phase_x)[None]
        sin_x = jnp.sin(phase_x)[None]
        weights = cotangent[freq]
        real_part = weights[0::2][:, None, :]
        imag_part = weights[1::2][:, None, :]
        first = real_part * cos_x - imag_part * sin_x
        second = -(real_part * sin_x + imag_part * cos_x)
        left = jnp.concatenate([first, second], axis=2).reshape(4 * rows_x, 2 * count)
        right = jnp.concatenate([jnp.cos(phase_y), jnp.sin(phase_y)], axis=1).T
        part = jnp.dot(
            left, right, preferred_element_type=jnp.float32, precision=lax.Precision.HIGHEST
        )
        return (total + part.reshape(4, rows_x, rows_y), None)

    start = jnp.zeros((4, rows_x, rows_y), jnp.float32)
    total, _ = lax.scan(one_freq, start, jnp.arange(cotangent.shape[0], dtype=jnp.int32))
    return total


def ahead(value, nearby, axis):
    rest = lax.slice_in_dim(value, 1, value.shape[axis], axis=axis)
    return jnp.concatenate([rest, nearby], axis) - value


def behind(value, nearby, axis):
    rest = lax.slice_in_dim(value, 0, value.shape[axis] - 1, axis=axis)
    return value - jnp.concatenate([nearby, rest], axis)


def local(
    e_field, h_field, pole_current, material, pole_table, cotangent, cosines, wavenumber, time_phase
):
    depth, width_x, width_y = material.shape
    scale = 1.0 / math.sqrt(DIRS * FREQS)
    anchor_x = (lax.axis_index("gx") * width_x).astype(jnp.float32)
    anchor_y = (lax.axis_index("gy") * width_y).astype(jnp.float32)
    ys = anchor_y + jnp.arange(width_y).astype(jnp.float32)
    first_cot, first_cos = turned_gather((cotangent, cosines), "gx", (2, 1))
    band_cot, band_cos = turned_gather((first_cot, first_cos), "gy", (2, 1))
    xs = anchor_x + jnp.arange(width_x).astype(jnp.float32)
    partial_value = surface_source(band_cot, band_cos, wavenumber, time_phase, xs, ys)
    source = of_everyone(partial_value, "gz") * scale
    is_top = lax.axis_index("gz") == lax.axis_size("gz") - 1
    top = ((jnp.arange(depth) == depth - 1) & is_top).astype(jnp.float32)[:, None, None]
    next_x = from_behind(e_field[1:3, :, :1, :], "gx", -1)
    next_y = from_behind(e_field[0::2, :, :, :1], "gy", -1)
    next_z = from_behind(e_field[0:2, :1], "gz", -1)
    ex, ey, ez = (e_field[0], e_field[1], e_field[2])
    curl_x = ahead(ez, next_y[1], 2) - ahead(ey, next_z[1], 0)
    curl_y = ahead(ex, next_z[0], 0) - ahead(ez, next_x[1], 1)
    curl_z = ahead(ey, next_x[0], 1) - ahead(ex, next_y[0], 2)
    hx = h_field[0] - courant * curl_x - courant * top * source[2][None]
    hy = h_field[1] - courant * curl_y - courant * top * source[3][None]
    hz = h_field[2] - courant * curl_z
    h_next = jnp.stack([hx, hy, hz])
    prev_x = from_behind(h_next[1:3, :, -1:, :], "gx", 1)
    prev_y = from_behind(h_next[0::2, :, :, -1:], "gy", 1)
    prev_z = from_behind(h_next[0:2, -1:], "gz", 1)
    chosen = (material[None] == jnp.arange(NPOLE, dtype=jnp.int32)[:, None, None, None]).astype(
        jnp.float32
    )
    decay = jnp.sum(chosen * pole_table[0][:, None, None, None], axis=0)
    drive = jnp.sum(chosen * pole_table[1][:, None, None, None], axis=0)
    coef = jnp.sum(chosen * pole_table[2][:, None, None, None], axis=0)
    pole_next = decay[None] * pole_current + drive[None] * e_field
    side_x = behind(hz, prev_y[1], 2) - behind(hy, prev_z[1], 0)
    side_y = behind(hx, prev_z[0], 0) - behind(hz, prev_x[1], 1)
    side_z = behind(hy, prev_x[0], 1) - behind(hx, prev_y[0], 2)
    curl_h = jnp.stack([side_x, side_y, side_z])
    inject = jnp.stack([top * source[0][None], top * source[1][None], jnp.zeros_like(ex)])
    e_next = (
        e_field + coef[None] * (curl_h - 0.5 * (pole_next + pole_current)) - coef[None] * inject
    )
    return (e_next, h_next, pole_next)


def solution(mesh):
    in_specs = (
        P(None, "gz", "gx", "gy"),
        P(None, "gz", "gx", "gy"),
        P(None, "gz", "gx", "gy"),
        P("gz", "gx", "gy"),
        P(),
        P(None, None, ("gx", "gy", "gz")),
        P(None, ("gx", "gy", "gz")),
        P(),
        P(),
    )
    out_specs = (P(None, "gz", "gx", "gy"), P(None, "gz", "gx", "gy"), P(None, "gz", "gx", "gy"))
    return jax.shard_map(local, mesh=mesh, in_specs=in_specs, out_specs=out_specs, check_vma=False)
```

profile of v0, /device:TPU:11, one launch (start us, length us, event | category | flops | bytes accessed | tf_op | source)
XLA Modules:
  0.0 227.1 jit_solution(3024068051090232866)
XLA Ops:
  2.2 11.3 %all_gather.6 = f32[32,130]{1,0:T(8,128)S(1)} all-gather(f32[8,130]{1,0:T(8,128)S(1)} %pad_maximum_fusion.2), channel_id=1, replica_groups=mesh['gx'=4,'gy'=16,'gz'=8] {'gx'}, dimensions={0}, use_global_device_ids=true | all-gather | bytes 20800 | tf_op jit(solution)/shard_map/all_gather | solution.py:17
  13.6 52.0 %all_gather.7 = f32[512,130]{1,0:T(8,128)S(1)} all-gather(f32[32,130]{1,0:T(8,128)S(1)} %all_gather.6), channel_id=1, replica_groups=mesh['gx'=4,'gy'=16,'gz'=8] {'gy'}, dimensions={0}, use_global_device_ids=true | all-gather | bytes 282880 | tf_op jit(solution)/shard_map/all_gather | solution.py:17
  66.6 106.9 %while.11 = (s32[]{:T(128)}, f32[4,32,128]{2,1,0:T(8,128)S(1)}, s32[16]{0:T(128)S(1)}, f32[16,8,512]{2,1,0:T(8,128)S(1)}, f32[16]{0:T(128)S(1)}, /*index=5*/f32[...) while((s32[]{:T(128)}, f32[4,32,128]{2,1,0:T(8,128)S(1)}, ...), condition=%wide.region_2.3_spmd.clone, body=%wide.region_1.2_spmd.clone.sunk | while | flops 202179904 | bytes 2586073 | solution.py:68
  70.6 0.9 fusion.51
  71.6 1.0 multiply_cosine_fusion.2
  77.3 0.9 fusion.51
  78.3 1.0 multiply_cosine_fusion.2
  84.0 0.9 fusion.51
  85.0 1.0 multiply_cosine_fusion.2
  91.7 1.0 multiply_cosine_fusion.2
  98.4 1.0 multiply_cosine_fusion.2
  105.0 1.0 multiply_cosine_fusion.2
  111.7 1.0 multiply_cosine_fusion.2
  118.4 1.0 multiply_cosine_fusion.2
  125.1 1.0 multiply_cosine_fusion.2
  131.8 1.0 multiply_cosine_fusion.2
  138.5 1.0 multiply_cosine_fusion.2
  145.1 1.0 multiply_cosine_fusion.2
  151.8 1.0 multiply_cosine_fusion.2
  158.5 1.0 multiply_cosine_fusion.2
  165.2 1.0 multiply_cosine_fusion.2
  171.9 1.0 multiply_cosine_fusion.2
  174.3 15.4 %all-to-all-start = ((f32[8,4,32,128]{3,2,1,0:T(8,128)}), f32[8,4,32,128]{3,2,1,0:T(8,128)S(1)}, u32[]{:S(2)}, u32[]{:S(2)}) async-start(f32[8,4,32,128]{3,2,1,0:T(8,128)} %broadcast_in_dim.5), calls=%async_computation | async-start | bytes 1048576 | tf_op jit(solution)/shard_map/all_to_all | solution.py:29
  189.8 5.1 %collective-permute-start.1 = (f32[2,4,32,1]{3,2,1,0:T(8,128)S(1)}, f32[2,4,32,1]{3,2,1,0:T(8,128)S(1)}, u32[]{:S(2)}, u32[]{:S(2)}) collective-permute-start(f32[2,4,32,1]{3,2,1,0:T(8,128)S(1)} %slice.160), channel_id=1, source_target_pairs={{8,0},{16,8},{24,16},{32,24},{40,32},{48,40},{56,48},{64,56},{72,6... | collective-permute-start | bytes 3080 | tf_op jit(solution)/shard_map/ppermute | solution.py:39
  194.9 2.5 %collective-permute-start.2 = (f32[2,1,32,128]{3,2,1,0:T(8,128)S(1)}, f32[2,1,32,128]{3,2,1,0:T(8,128)S(1)}, u32[]{:S(2)}, u32[]{:S(2)}) collective-permute-start(f32[2,1,32,128]{3,2,1,0:T(8,128)S(1)} %slice.167), channel_id=1, source_target_pairs={{1,0},{2,1},{3,2},{4,3},{5,4},{6,5},{7,6},{9,8},{10,9},{11,10},{12... | collective-permute-start | bytes 98312 | tf_op jit(solution)/shard_map/ppermute | solution.py:39
  197.5 1.3 collective-permute-start
  200.0 6.9 %collective-permute-done.1 = f32[2,4,32,1]{3,2,1,0:T(8,128)S(1)} collective-permute-done((f32[2,4,32,1]{3,2,1,0:T(8,128)S(1)}, f32[2,4,32,1]{3,2,1,0:T(8,128)S(1)}, u32[]{:S(2)}, u32[]{:S(2)}) %collective-permute-start.1) | collective-permute-done | bytes 1056 | tf_op jit(solution)/shard_map/ppermute | solution.py:39
  207.1 0.9 copy-done.1
  209.1 2.3 %collective-permute-start.3 = (f32[2,4,32,1]{3,2,1,0:T(8,128)S(1)}, f32[2,4,32,1]{3,2,1,0:T(8,128)S(1)}, u32[]{:S(2)}, u32[]{:S(2)}) collective-permute-start(f32[2,4,32,1]{3,2,1,0:T(8,128)S(1)} %slice.176), channel_id=1, source_target_pairs={{0,8},{8,16},{16,24},{24,32},{32,40},{40,48},{48,56},{56,64},{64,7... | collective-permute-start | bytes 3080 | tf_op jit(solution)/shard_map/ppermute | solution.py:39
  211.4 1.3 collective-permute-start.5
  212.7 5.2 %collective-permute-start.4 = (f32[2,1,32,128]{3,2,1,0:T(8,128)S(1)}, f32[2,1,32,128]{3,2,1,0:T(8,128)S(1)}, u32[]{:S(2)}, u32[]{:S(2)}) collective-permute-start(f32[2,1,32,128]{3,2,1,0:T(8,128)S(1)} %pad_maximum_fusion.1), channel_id=1, source_target_pairs={{0,1},{1,2},{2,3},{3,4},{4,5},{5,6},{6,7},{8,9},{9,10},{10,11},{11... | collective-permute-start | bytes 98312 | tf_op jit(solution)/shard_map/ppermute | solution.py:39
  218.0 7.3 %collective-permute-done.3 = f32[2,4,32,1]{3,2,1,0:T(8,128)S(1)} collective-permute-done((f32[2,4,32,1]{3,2,1,0:T(8,128)S(1)}, f32[2,4,32,1]{3,2,1,0:T(8,128)S(1)}, u32[]{:S(2)}, u32[]{:S(2)}) %collective-permute-start.3) | collective-permute-done | bytes 1056 | tf_op jit(solution)/shard_map/ppermute | solution.py:39
  (259 shorter events, 67.7 us)
Async XLA Ops:
  1.5 0.7 copy-start.6
  65.9 0.7 copy-start.7
  65.9 0.7 copy-start.8
  174.3 15.4 %copy-start = (f32[3,4,32,128]{3,2,1,0:T(8,128)S(1)}, f32[3,4,32,128]{3,2,1,0:T(8,128)}, u32[]{:S(2)}) copy-start(f32[3,4,32,128]{3,2,1,0:T(8,128)} %param.11) | copy-start | bytes 589828
  174.3 32.6 %all-to-all-start = ((f32[8,4,32,128]{3,2,1,0:T(8,128)}), f32[8,4,32,128]{3,2,1,0:T(8,128)S(1)}, u32[]{:S(2)}, u32[]{:S(2)}) async-start(f32[8,4,32,128]{3,2,1,0:T(8,128)} %broadcast_in_dim.5), calls=%async_computation | async-start | bytes 1048576 | tf_op jit(solution)/shard_map/all_to_all | solution.py:29
  189.8 17.1 %collective-permute-start.1 = (f32[2,4,32,1]{3,2,1,0:T(8,128)S(1)}, f32[2,4,32,1]{3,2,1,0:T(8,128)S(1)}, u32[]{:S(2)}, u32[]{:S(2)}) collective-permute-start(f32[2,4,32,1]{3,2,1,0:T(8,128)S(1)} %slice.160), channel_id=1, source_target_pairs={{8,0},{16,8},{24,16},{32,24},{40,32},{48,40},{56,48},{64,56},{72,6... | collective-permute-start | bytes 3080 | tf_op jit(solution)/shard_map/ppermute | solution.py:39
  194.9 12.0 %collective-permute-start.2 = (f32[2,1,32,128]{3,2,1,0:T(8,128)S(1)}, f32[2,1,32,128]{3,2,1,0:T(8,128)S(1)}, u32[]{:S(2)}, u32[]{:S(2)}) collective-permute-start(f32[2,1,32,128]{3,2,1,0:T(8,128)S(1)} %slice.167), channel_id=1, source_target_pairs={{1,0},{2,1},{3,2},{4,3},{5,4},{6,5},{7,6},{9,8},{10,9},{11,10},{12... | collective-permute-start | bytes 98312 | tf_op jit(solution)/shard_map/ppermute | solution.py:39
  197.5 9.5 %collective-permute-start = (f32[2,4,1,128]{3,2,1,0:T(1,128)S(1)}, f32[2,4,1,128]{3,2,1,0:T(1,128)S(1)}, u32[]{:S(2)}, u32[]{:S(2)}) collective-permute-start(f32[2,4,1,128]{3,2,1,0:T(1,128)S(1)} %slice.156), channel_id=1, source_target_pairs={{128,0},{256,128},{384,256},{129,1},{257,129},{385,257},{130,2},{2... | collective-permute-start | bytes 12296 | tf_op jit(solution)/shard_map/ppermute | solution.py:39
  198.9 0.8 copy-start.4
  198.9 0.7 copy-start.5
  207.0 0.9 copy-start.1
  208.3 0.7 copy-start.2
  209.1 16.2 %collective-permute-start.3 = (f32[2,4,32,1]{3,2,1,0:T(8,128)S(1)}, f32[2,4,32,1]{3,2,1,0:T(8,128)S(1)}, u32[]{:S(2)}, u32[]{:S(2)}) collective-permute-start(f32[2,4,32,1]{3,2,1,0:T(8,128)S(1)} %slice.176), channel_id=1, source_target_pairs={{0,8},{8,16},{16,24},{24,32},{32,40},{40,48},{48,56},{56,64},{64,7... | collective-permute-start | bytes 3080 | tf_op jit(solution)/shard_map/ppermute | solution.py:39
  211.4 13.9 %collective-permute-start.5 = (f32[2,4,1,128]{3,2,1,0:T(1,128)S(1)}, f32[2,4,1,128]{3,2,1,0:T(1,128)S(1)}, u32[]{:S(2)}, u32[]{:S(2)}) collective-permute-start(f32[2,4,1,128]{3,2,1,0:T(1,128)S(1)} %pad_maximum_fusion.3), channel_id=1, source_target_pairs={{0,128},{128,256},{256,384},{1,129},{129,257},{257,385},{2,130},{1... | collective-permute-start | bytes 12296 | tf_op jit(solution)/shard_map/ppermute | solution.py:39
  212.7 12.6 %collective-permute-start.4 = (f32[2,1,32,128]{3,2,1,0:T(8,128)S(1)}, f32[2,1,32,128]{3,2,1,0:T(8,128)S(1)}, u32[]{:S(2)}, u32[]{:S(2)}) collective-permute-start(f32[2,1,32,128]{3,2,1,0:T(8,128)S(1)} %pad_maximum_fusion.1), channel_id=1, source_target_pairs={{0,1},{1,2},{2,3},{3,4},{4,5},{5,6},{6,7},{8,9},{9,10},{10,11},{11... | collective-permute-start | bytes 98312 | tf_op jit(solution)/shard_map/ppermute | solution.py:39
  225.3 0.9 copy-start.3
where the time goes:
time: 228 us; the launch traced here: 227 us
  blocking collectives  63.3 us (28%)
  other arithmetic  41.8 us (18%)
  local copies, waits for them, and re-layouts  35.4 us (16%)
  starting transfers between devices  33.1 us (15%)
  loops' own time  28.5 us (12%)
  waiting for transfers between devices  14.2 us (6%)
  matrix products  9.66 us (4%)
    all_gather x2, blocking collectives, turned_gather(): filled = lax.all_gather(both, axis, axis=0, tiled=True)  63.3 us
    another operation x1, loops' own time, surface_source(): lax.scan(one_freq, start, jnp.arange(cotangent.shape[0], dtype=jnp.int32))  28.5 us
    ppermute x6, starting transfers between devices, from_behind(): return lax.ppermute(array, axis, pairs)  17.7 us
    cos x16, other arithmetic, one_freq(): right = jnp.concatenate([jnp.cos(phase_y), jnp.sin(phase_y)], axis=1).T  15.7 us
    all_to_all x1, starting transfers between devices, copy_for_each(): return lax.all_to_all(copies, axis, split_axis=0, concat_axis=0, tiled=True)  15.4 us
    ppermute x6, waiting for transfers between devices, from_behind(): return lax.ppermute(array, axis, pairs)  14.2 us
    cos x16, other arithmetic, one_freq(): cos_x = jnp.cos(phase_x)[None]  14 us
    dot_general x16, matrix products, one_freq(): jnp.dot(left, right, preferred_element_type=jnp.float32, precision=lax.Pr...  9.66 us
  transfers between devices with their start and end apart: 7, of which 2 were waited for; matrix products, arithmetic and copies ran while one was open for 0% of the time, Pallas kernels for 0%

commit v1 on v0

--- a/solution.py
+++ b/solution.py
@@ -14,7 +14,9 @@
     turned = [jnp.moveaxis(a, dim, 0) for a, dim in zip(arrays, dims)]
     widths = [t[0].size for t in turned]
     both = jnp.concatenate([t.reshape(-1, w) for t, w in zip(turned, widths)], axis=1)
-    filled = lax.all_gather(both, axis, axis=0, tiled=True)
+    filled = jnp.concatenate(
+        lax.all_to_all(jnp.stack([both] * lax.axis_size(axis)), axis, 0, 0), axis=0
+    )
     tiles = jnp.split(filled, [sum(widths[:k]) for k in range(1, len(widths))], axis=1)
     return tuple(
         (

time: 228 us -> 221 us (0.969)
  the two profiles are of different devices: /device:TPU:11 before, /device:TPU:3 now
where the time goes in v1:
time: 221 us; the launch traced here: 220 us
  waiting for transfers between devices  54.8 us (25%)
  other arithmetic  44.3 us (20%)
  starting transfers between devices  40.6 us (18%)
  local copies, waits for them, and re-layouts  37.2 us (17%)
  loops' own time  32.2 us (15%)
  matrix products  9.69 us (4%)
    all_to_all x2, waiting for transfers between devices, turned_gather(): lax.all_to_all(jnp.stack([both] * lax.axis_size(axis)), axis, 0, 0)  33.5 us
    another operation x1, loops' own time, surface_source(): lax.scan(one_freq, start, jnp.arange(cotangent.shape[0], dtype=jnp.int32))  32.2 us
    ppermute x6, starting transfers between devices, from_behind(): return lax.ppermute(array, axis, pairs)  21.9 us
    cos x16, other arithmetic, one_freq(): right = jnp.concatenate([jnp.cos(phase_y), jnp.sin(phase_y)], axis=1).T  15.7 us
    cos x16, other arithmetic, one_freq(): cos_x = jnp.cos(phase_x)[None]  15.3 us
    all_to_all x2, starting transfers between devices, turned_gather(): lax.all_to_all(jnp.stack([both] * lax.axis_size(axis)), axis, 0, 0)  13.7 us
    ppermute x6, waiting for transfers between devices, from_behind(): return lax.ppermute(array, axis, pairs)  11.9 us
    mul x16, other arithmetic, one_freq(): along_y = wave * cosines[1]  10.4 us
  transfers between devices with their start and end apart: 9, of which 3 were waited for; matrix products, arithmetic and copies ran while one was open for 38% of the time, Pallas kernels for 0%

profile of v1, /device:TPU:3, one launch (start us, length us, event | category | flops | bytes accessed | tf_op | source)
XLA Modules:
  0.0 219.9 jit_solution(6362701195088469926)
XLA Ops:
  3.0 5.6 %all-to-all-start = ((f32[4,8,130]{2,1,0:T(8,128)}), f32[4,8,130]{2,1,0:T(8,128)S(1)}, u32[]{:S(2)}, u32[]{:S(2)}) async-start(f32[4,8,130]{2,1,0:T(8,128)} %stack.16), calls=%async_computation | async-start | bytes 65536 | tf_op jit(solution)/shard_map/all_to_all | solution.py:18
  8.6 10.2 %collective-permute-start.1 = (f32[2,4,32,1]{3,2,1,0:T(8,128)S(1)}, f32[2,4,32,1]{3,2,1,0:T(8,128)S(1)}, u32[]{:S(2)}, u32[]{:S(2)}) collective-permute-start(f32[2,4,32,1]{3,2,1,0:T(8,128)S(1)} %slice.160), channel_id=1, source_target_pairs={{8,0},{16,8},{24,16},{32,24},{40,32},{48,40},{56,48},{64,56},{72,6... | collective-permute-start | bytes 3080 | tf_op jit(solution)/shard_map/ppermute | solution.py:41
  18.9 2.9 %collective-permute-start.2 = (f32[2,1,32,128]{3,2,1,0:T(8,128)S(1)}, f32[2,1,32,128]{3,2,1,0:T(8,128)S(1)}, u32[]{:S(2)}, u32[]{:S(2)}) collective-permute-start(f32[2,1,32,128]{3,2,1,0:T(8,128)S(1)} %slice.167), channel_id=1, source_target_pairs={{1,0},{2,1},{3,2},{4,3},{5,4},{6,5},{7,6},{9,8},{10,9},{11,10},{12... | collective-permute-start | bytes 98312 | tf_op jit(solution)/shard_map/ppermute | solution.py:41
  21.8 1.3 collective-permute-start
  24.9 8.1 %all-to-all-start.1 = ((f32[16,32,130]{2,1,0:T(8,128)}), f32[16,32,130]{2,1,0:T(8,128)S(1)}, u32[]{:S(2)}, u32[]{:S(2)}) async-start(f32[16,32,130]{2,1,0:T(8,128)} %stack.18), calls=%async_computation.1 | async-start | bytes 1048576 | tf_op jit(solution)/shard_map/all_to_all | solution.py:18
  33.1 33.5 %all-to-all-done.1 = f32[16,32,130]{2,1,0:T(8,128)S(1)} async-done(((f32[16,32,130]{2,1,0:T(8,128)}), f32[16,32,130]{2,1,0:T(8,128)S(1)}, u32[]{:S(2)}, u32[]{:S(2)}) %all-to-all-start.1) | async-done | bytes 266272 | tf_op jit(solution)/shard_map/all_to_all | solution.py:18
  67.6 113.6 %while.11 = (s32[]{:T(128)}, f32[4,32,128]{2,1,0:T(8,128)S(1)}, s32[16]{0:T(128)S(1)}, f32[16,8,512]{2,1,0:T(8,128)S(1)}, f32[16]{0:T(128)S(1)}, /*index=5*/f32[...) while((s32[]{:T(128)}, f32[4,32,128]{2,1,0:T(8,128)S(1)}, ...), condition=%wide.region_2.3_spmd.clone, body=%wide.region_1.2_spmd.clone.sunk | while | flops 202179904 | bytes 2586073 | solution.py:70
  72.0 1.0 fusion.51
  73.1 1.0 multiply_cosine_fusion.2
  80.2 1.0 multiply_cosine_fusion.2
  87.3 1.0 multiply_cosine_fusion.2
  93.3 1.0 fusion.51
  94.4 1.0 multiply_cosine_fusion.2
  101.5 1.0 multiply_cosine_fusion.2
  108.6 1.0 multiply_cosine_fusion.2
  115.7 1.0 multiply_cosine_fusion.2
  122.8 1.0 multiply_cosine_fusion.2
  128.8 1.0 fusion.51
  129.9 1.0 multiply_cosine_fusion.2
  137.0 1.0 multiply_cosine_fusion.2
  144.1 1.0 multiply_cosine_fusion.2
  151.2 1.0 multiply_cosine_fusion.2
  158.3 1.0 multiply_cosine_fusion.2
  165.4 1.0 multiply_cosine_fusion.2
  172.5 1.0 multiply_cosine_fusion.2
  179.6 1.0 multiply_cosine_fusion.2
  182.0 5.0 %all-to-all-start.2 = ((f32[8,4,32,128]{3,2,1,0:T(8,128)}), f32[8,4,32,128]{3,2,1,0:T(8,128)S(1)}, u32[]{:S(2)}, u32[]{:S(2)}) async-start(f32[8,4,32,128]{3,2,1,0:T(8,128)} %broadcast_in_dim.5), calls=%async_computation.2 | async-start | bytes 1048576 | tf_op jit(solution)/shard_map/all_to_all | solution.py:31
  187.1 9.4 %all-to-all-done.2 = f32[8,4,32,128]{3,2,1,0:T(8,128)S(1)} async-done(((f32[8,4,32,128]{3,2,1,0:T(8,128)}), f32[8,4,32,128]{3,2,1,0:T(8,128)S(1)}, u32[]{:S(2)}, u32[]{:S(2)}) %all-to-all-start.2) | async-done | bytes 524320 | tf_op jit(solution)/shard_map/all_to_all | solution.py:31
  198.6 1.9 collective-permute-start.3
  200.6 2.3 %collective-permute-start.5 = (f32[2,4,1,128]{3,2,1,0:T(1,128)S(1)}, f32[2,4,1,128]{3,2,1,0:T(1,128)S(1)}, u32[]{:S(2)}, u32[]{:S(2)}) collective-permute-start(f32[2,4,1,128]{3,2,1,0:T(1,128)S(1)} %pad_maximum_fusion.3), channel_id=1, source_target_pairs={{0,128},{128,256},{256,384},{1,129},{129,257},{257,385},{2,130},{1... | collective-permute-start | bytes 12296 | tf_op jit(solution)/shard_map/ppermute | solution.py:41
  202.9 3.3 %collective-permute-start.4 = (f32[2,1,32,128]{3,2,1,0:T(8,128)S(1)}, f32[2,1,32,128]{3,2,1,0:T(8,128)S(1)}, u32[]{:S(2)}, u32[]{:S(2)}) collective-permute-start(f32[2,1,32,128]{3,2,1,0:T(8,128)S(1)} %pad_maximum_fusion.1), channel_id=1, source_target_pairs={{0,1},{1,2},{2,3},{3,4},{4,5},{5,6},{6,7},{8,9},{9,10},{10,11},{11... | collective-permute-start | bytes 98312 | tf_op jit(solution)/shard_map/ppermute | solution.py:41
  206.2 11.8 %collective-permute-done.3 = f32[2,4,32,1]{3,2,1,0:T(8,128)S(1)} collective-permute-done((f32[2,4,32,1]{3,2,1,0:T(8,128)S(1)}, f32[2,4,32,1]{3,2,1,0:T(8,128)S(1)}, u32[]{:S(2)}, u32[]{:S(2)}) %collective-permute-start.3) | collective-permute-done | bytes 1056 | tf_op jit(solution)/shard_map/ppermute | solution.py:41
  (261 shorter events, 72.7 us)
Async XLA Ops:
  0.6 8.0 %copy-start = (f32[3,4,32,128]{3,2,1,0:T(8,128)S(1)}, f32[3,4,32,128]{3,2,1,0:T(8,128)}, u32[]{:S(2)}) copy-start(f32[3,4,32,128]{3,2,1,0:T(8,128)} %param.11) | copy-start | bytes 589828
  3.0 21.0 %all-to-all-start = ((f32[4,8,130]{2,1,0:T(8,128)}), f32[4,8,130]{2,1,0:T(8,128)S(1)}, u32[]{:S(2)}, u32[]{:S(2)}) async-start(f32[4,8,130]{2,1,0:T(8,128)} %stack.16), calls=%async_computation | async-start | bytes 65536 | tf_op jit(solution)/shard_map/all_to_all | solution.py:18
  8.6 15.1 %copy-start.4 = (s32[4,32,128]{2,1,0:T(8,128)S(1)}, s32[4,32,128]{2,1,0:T(8,128)}, u32[]{:S(2)}) copy-start(s32[4,32,128]{2,1,0:T(8,128)} %param.14) | copy-start | bytes 196612
  8.6 178.4 %collective-permute-start.1 = (f32[2,4,32,1]{3,2,1,0:T(8,128)S(1)}, f32[2,4,32,1]{3,2,1,0:T(8,128)S(1)}, u32[]{:S(2)}, u32[]{:S(2)}) collective-permute-start(f32[2,4,32,1]{3,2,1,0:T(8,128)S(1)} %slice.160), channel_id=1, source_target_pairs={{8,0},{16,8},{24,16},{32,24},{40,32},{48,40},{56,48},{64,56},{72,6... | collective-permute-start | bytes 3080 | tf_op jit(solution)/shard_map/ppermute | solution.py:41
  18.9 168.2 %collective-permute-start.2 = (f32[2,1,32,128]{3,2,1,0:T(8,128)S(1)}, f32[2,1,32,128]{3,2,1,0:T(8,128)S(1)}, u32[]{:S(2)}, u32[]{:S(2)}) collective-permute-start(f32[2,1,32,128]{3,2,1,0:T(8,128)S(1)} %slice.167), channel_id=1, source_target_pairs={{1,0},{2,1},{3,2},{4,3},{5,4},{6,5},{7,6},{9,8},{10,9},{11,10},{12... | collective-permute-start | bytes 98312 | tf_op jit(solution)/shard_map/ppermute | solution.py:41
  21.8 165.3 %collective-permute-start = (f32[2,4,1,128]{3,2,1,0:T(1,128)S(1)}, f32[2,4,1,128]{3,2,1,0:T(1,128)S(1)}, u32[]{:S(2)}, u32[]{:S(2)}) collective-permute-start(f32[2,4,1,128]{3,2,1,0:T(1,128)S(1)} %slice.156), channel_id=1, source_target_pairs={{128,0},{256,128},{384,256},{129,1},{257,129},{385,257},{130,2},{2... | collective-permute-start | bytes 12296 | tf_op jit(solution)/shard_map/ppermute | solution.py:41
  23.1 0.7 copy-start.5
  24.9 41.8 %all-to-all-start.1 = ((f32[16,32,130]{2,1,0:T(8,128)}), f32[16,32,130]{2,1,0:T(8,128)S(1)}, u32[]{:S(2)}, u32[]{:S(2)}) async-start(f32[16,32,130]{2,1,0:T(8,128)} %stack.18), calls=%async_computation.1 | async-start | bytes 1048576 | tf_op jit(solution)/shard_map/all_to_all | solution.py:18
  66.9 0.7 copy-start.6
  66.9 0.7 copy-start.7
  182.0 14.5 %all-to-all-start.2 = ((f32[8,4,32,128]{3,2,1,0:T(8,128)}), f32[8,4,32,128]{3,2,1,0:T(8,128)S(1)}, u32[]{:S(2)}, u32[]{:S(2)}) async-start(f32[8,4,32,128]{3,2,1,0:T(8,128)} %broadcast_in_dim.5), calls=%async_computation.2 | async-start | bytes 1048576 | tf_op jit(solution)/shard_map/all_to_all | solution.py:31
  196.6 0.9 copy-start.1
  197.8 0.7 copy-start.2
  198.6 19.4 %collective-permute-start.3 = (f32[2,4,32,1]{3,2,1,0:T(8,128)S(1)}, f32[2,4,32,1]{3,2,1,0:T(8,128)S(1)}, u32[]{:S(2)}, u32[]{:S(2)}) collective-permute-start(f32[2,4,32,1]{3,2,1,0:T(8,128)S(1)} %slice.176), channel_id=1, source_target_pairs={{0,8},{8,16},{16,24},{24,32},{32,40},{40,48},{48,56},{56,64},{64,7... | collective-permute-start | bytes 3080 | tf_op jit(solution)/shard_map/ppermute | solution.py:41
  200.6 17.5 %collective-permute-start.5 = (f32[2,4,1,128]{3,2,1,0:T(1,128)S(1)}, f32[2,4,1,128]{3,2,1,0:T(1,128)S(1)}, u32[]{:S(2)}, u32[]{:S(2)}) collective-permute-start(f32[2,4,1,128]{3,2,1,0:T(1,128)S(1)} %pad_maximum_fusion.3), channel_id=1, source_target_pairs={{0,128},{128,256},{256,384},{1,129},{129,257},{257,385},{2,130},{1... | collective-permute-start | bytes 12296 | tf_op jit(solution)/shard_map/ppermute | solution.py:41
  202.9 15.2 %collective-permute-start.4 = (f32[2,1,32,128]{3,2,1,0:T(8,128)S(1)}, f32[2,1,32,128]{3,2,1,0:T(8,128)S(1)}, u32[]{:S(2)}, u32[]{:S(2)}) collective-permute-start(f32[2,1,32,128]{3,2,1,0:T(8,128)S(1)} %pad_maximum_fusion.1), channel_id=1, source_target_pairs={{0,1},{1,2},{2,3},{3,4},{4,5},{5,6},{6,7},{8,9},{9,10},{10,11},{11... | collective-permute-start | bytes 98312 | tf_op jit(solution)/shard_map/ppermute | solution.py:41
  218.1 0.9 copy-start.3
